TPU v7x, 32 devices: a whole 2x2x4 slice. The times are simulated.
32 devices in a mesh: grp: 2 (over y), ex: 8 (over z, x), tp: 2 (over core).
Axes of the slice: x: 2, y: 2, z: 4, core: 2. Of those that a mesh axis runs over, the one named last changes fastest.
Arguments:
- hidden_states: bfloat16 [64, 3584], P(('grp', 'ex')), parts along dimension 0
- draft_row: int32 [64], P(('grp', 'ex')), parts along dimension 0, may hold values from 0 to 31, as said below
- expert_ids: int32 [2, 64, 8], P(None, ('grp', 'ex')), parts along dimension 1, may hold values from 0 to 7, all different within a row; in each aligned block of 4 rows (0 to 3, 4 to 7, ..., all dimensions but the last counted through in order) at most 4 rows name the same one
- route_weights: float32 [2, 64, 8], P(None, ('grp', 'ex')), parts along dimension 1, may hold values from 0.1 to 0.6
- norm_gain: float32 [3584], replicated, may hold values from 0.1 to 1.9
- w_gate: bfloat16 [3584, 8192], P(None, ('ex', 'tp')), may hold values from -0.09375 to 0.09375
- w_up: bfloat16 [3584, 8192], P(None, ('ex', 'tp')), may hold values from -0.09375 to 0.09375
- w_down: bfloat16 [8192, 3584], P(('ex', 'tp')), may hold values from -0.1875 to 0.1875
Outputs:
- draft_hidden: bfloat16 [64, 3584], P(('grp', 'ex')), parts along dimension 0
There are 2 independent parts, one for each index of `grp`. A program takes and returns all parts, laid end to end along the dimension named above; an argument that names none is the same for every part. Nothing has to cross between parts.
Inputs may be any that keep to these rules, and one draw needn't show every extreme that they name: draft_row is a permutation of the 32 rows; draft row r lies on index r // 4 of ex; the 4 decode rows of one index go to at most 2 rows of any one draft index, and some pairs reach 2. `expert_ids`: each row names 8 different experts; of the 4 rows of one index of ex in one step, at most 4 name the same expert, and some expert reaches 4.
All inputs are finite; a program needn't handle non-finite values.
Results may differ from a plain program's by a relative error of at most 0.019.
Values may be sent and summed in bfloat16 or wider, within the bound.
A program may use at most 64 MiB of HBM per device.

v0:
```python
import jax
import jax.numpy as jnp
from jax import lax
from jax.sharding import PartitionSpec as P

HID = 1024
STEPS = 2
RCAP = 2


epsilon = 1e-06


def expert_block(rows_in, w_gate, w_up, w_down):
    gate_proj = jnp.dot(rows_in, w_gate, preferred_element_type=jnp.float32)
    up_proj = jnp.dot(rows_in, w_up, preferred_element_type=jnp.float32)
    activated = (jax.nn.silu(gate_proj) * up_proj).astype(jnp.bfloat16)
    return jnp.dot(activated, w_down, preferred_element_type=jnp.float32)


def fold_back(returned, seating, route_coef, experts, group_size):
    ex_size, slot_cap, columns = returned.shape
    summed = returned.reshape(experts, group_size, slot_cap, columns).sum(axis=1)
    scale = seating.astype(jnp.float32) * route_coef.T[:, None, :]
    return jnp.einsum(
        "ecr,ecd->rd",
        scale,
        summed,
        precision=lax.Precision.HIGHEST,
        preferred_element_type=jnp.float32,
    )


def shards(hidden_states, draft_row, expert_ids, route_weights, norm_gain, w_gate, w_up, w_down):
    row_dev, features = hidden_states.shape
    ex_size = lax.axis_size("ex")
    tp_size = lax.axis_size("tp")
    hid_dev = w_gate.shape[1]
    group_size = HID // (hid_dev * tp_size)
    experts = ex_size // group_size
    chosen_count = expert_ids.shape[2]
    slot_cap = min(row_dev, max(2, 2 * row_dev * chosen_count // experts))
    target_dev = draft_row // row_dev
    target_pos = draft_row % row_dev
    same_dest = target_dev[:, None] == target_dev[None, :]
    earlier = jnp.tril(jnp.ones((row_dev, row_dev), jnp.bool_), -1)
    order_in = jnp.sum(same_dest & earlier, axis=1)
    slot_index = target_dev * RCAP + order_in
    picker = jnp.arange(ex_size * RCAP, dtype=jnp.int32)[:, None] == slot_index[None, :]
    outgoing = (
        jnp.dot(picker.astype(jnp.bfloat16), hidden_states, preferred_element_type=jnp.float32)
        .astype(jnp.bfloat16)
        .reshape(ex_size, RCAP, features)
    )
    labels = (
        jnp.sum(jnp.where(picker, target_pos[None, :] + 1, 0), axis=1)
        .astype(jnp.bfloat16)
        .reshape(ex_size, RCAP)
    )
    arrived, arrived_labels = (
        lax.all_to_all(outgoing, "ex", split_axis=0, concat_axis=0, tiled=True),
        lax.all_to_all(labels, "ex", split_axis=0, concat_axis=0, tiled=True),
    )
    arrived = arrived.reshape(ex_size * RCAP, features)
    settle = (
        arrived_labels.reshape(-1).astype(jnp.float32)[None, :]
        == (jnp.arange(row_dev) + 1).astype(jnp.float32)[:, None]
    )
    current = jnp.dot(
        settle.astype(jnp.bfloat16), arrived, preferred_element_type=jnp.float32
    ).astype(jnp.bfloat16)
    slot_total = ex_size * slot_cap
    for step_no in range(STEPS):
        as_float = current.astype(jnp.float32)
        mean_square = jnp.mean(as_float * as_float, axis=-1, keepdims=True)
        normed = (as_float * lax.rsqrt(mean_square + epsilon) * norm_gain).astype(jnp.bfloat16)
        step_ids = expert_ids[step_no]
        weights = route_weights[step_no]
        matches = step_ids[:, :, None] == jnp.arange(experts, dtype=jnp.int32)[None, None, :]
        chosen = jnp.any(matches, axis=1)
        route_coef = jnp.sum(jnp.where(matches, weights[:, :, None], 0.0), axis=1)
        chosen_int = chosen.astype(jnp.int32)
        before = jnp.cumsum(chosen_int, axis=0) - chosen_int
        seating = chosen.T[:, None, :] & (
            before.T[:, None, :] == jnp.arange(slot_cap, dtype=jnp.int32)[None, :, None]
        )
        packed_base = jnp.einsum(
            "ecr,rd->ecd", seating.astype(jnp.bfloat16), normed, preferred_element_type=jnp.float32
        ).astype(jnp.bfloat16)
        occupancy = jnp.any(seating, axis=2).astype(jnp.bfloat16)
        occupancy = jnp.broadcast_to(occupancy[:, None], (experts, group_size, slot_cap)).reshape(
            ex_size, slot_cap
        )
        packed = jnp.broadcast_to(
            packed_base[:, None], (experts, group_size, slot_cap, features)
        ).reshape(ex_size, slot_cap, features)
        landed, landed_flags = (
            lax.all_to_all(packed, "ex", split_axis=0, concat_axis=0, tiled=True),
            lax.all_to_all(occupancy, "ex", split_axis=0, concat_axis=0, tiled=True),
        )
        rows_in = landed.reshape(slot_total, features)
        partial_value = expert_block(rows_in, w_gate, w_up, w_down)
        returned = lax.all_to_all(
            partial_value.reshape(ex_size, slot_cap, features).astype(jnp.bfloat16),
            "ex",
            split_axis=0,
            concat_axis=0,
            tiled=True,
        ).astype(jnp.float32)
        branch_sum = lax.psum(
            fold_back(returned, seating, route_coef, experts, group_size).astype(jnp.bfloat16), "tp"
        ).astype(jnp.float32)
        current = (current.astype(jnp.float32) + branch_sum).astype(jnp.bfloat16)
    return current


def solution(mesh):
    in_specs = (
        P(("grp", "ex"), None),
        P(("grp", "ex")),
        P(None, ("grp", "ex"), None),
        P(None, ("grp", "ex"), None),
        P(),
        P(None, ("ex", "tp")),
        P(None, ("ex", "tp")),
        P(("ex", "tp"), None),
    )
    out_specs = P(("grp", "ex"), None)
    return jax.shard_map(shards, mesh=mesh, in_specs=in_specs, out_specs=out_specs, check_vma=False)
```

profile of v0, /device:TPU:0, one launch (start us, length us, event | category | flops | bytes accessed | tf_op | source)
XLA Modules:
  0.0 99.3 jit_solution(12188095769534011482)
XLA Ops:
  0.0 0.0 copy-start
  0.0 0.7 fusion.58
  0.7 0.2 convert_reduce_fusion.1
  0.9 0.1 select_reduce_fusion.2
  1.0 0.7 convert_element_type.147
  1.7 7.3 %all-to-all-start = ((bf16[8,1,2]{2,1,0:T(2,128)(2,1)}), bf16[8,1,2]{2,1,0:T(2,128)(2,1)S(1)}, u32[]{:S(2)}, u32[]{:S(2)}) async-start(bf16[8,1,2]{2,1,0:T(2,128)(2,1)} %convert_element_type.147), calls=%async_computation | async-start | bytes 8192 | tf_op jit(solution)/shard_map/all_to_all | solution.py:62
  8.9 0.0 copy-done
  8.9 0.3 convolution_convert_fusion.4
  9.2 0.7 slice_bitcast_fusion.1
  9.9 0.1 fusion.32
  10.1 0.7 reshape.83
  10.7 4.5 %all-to-all-done = bf16[8,1,2]{2,1,0:T(2,128)(2,1)S(1)} async-done(((bf16[8,1,2]{2,1,0:T(2,128)(2,1)}), bf16[8,1,2]{2,1,0:T(2,128)(2,1)S(1)}, u32[]{:S(2)}, u32[]{:S(2)}) %all-to-all-start) | async-done | bytes 64 | tf_op jit(solution)/shard_map/all_to_all | solution.py:62
  15.3 3.4 %all-to-all-start.1 = ((bf16[8,2,3584]{2,1,0:T(2,128)(2,1)}), bf16[8,2,3584]{2,1,0:T(2,128)(2,1)S(1)}, u32[]{:S(2)}, u32[]{:S(2)}) async-start(bf16[8,2,3584]{2,1,0:T(2,128)(2,1)} %reshape.83), calls=%async_computation.1 | async-start | bytes 229376 | tf_op jit(solution)/shard_map/all_to_all | solution.py:61
  18.7 0.1 reshape.87
  18.8 7.1 %all-to-all-done.1 = bf16[8,2,3584]{2,1,0:T(2,128)(2,1)S(1)} async-done(((bf16[8,2,3584]{2,1,0:T(2,128)(2,1)}), bf16[8,2,3584]{2,1,0:T(2,128)(2,1)S(1)}, u32[]{:S(2)}, u32[]{:S(2)}) %all-to-all-start.1) | async-done | bytes 114720 | tf_op jit(solution)/shard_map/all_to_all | solution.py:61
  25.9 0.3 multiply_reduce_fusion
  26.2 1.0 %convolution_convert_fusion.3 = bf16[8,4,3584]{2,0,1:T(8,128)(2,1)S(1)} fusion(f32[4,3584]{1,0:T(4,128)S(1)} %get-tuple-element.14, f32[3584]{0:T(1024)} %param.12, f32[4]{0:T(128)S(1)} %add_rsqrt_fusion.1, s32[8,4]{0,1:T(4,128)S(1)} %bitcast_subtract_fusion.1, pred[8,4]{0,1:T(4,128)(4,1)S(1)} %bitcast.44), kind=kOutput, calls=%fused_computation.3 | convolution fusion | flops 1075456 | bytes 301232 | tf_op jit(solution)/shard_map/ecr,rd->ecd/dot_general | solution.py:87
  27.2 0.8 copy.21
  28.0 3.4 %all-to-all-start.2 = ((bf16[8,4,3584]{2,1,0:T(4,128)(2,1)}), bf16[8,4,3584]{2,1,0:T(4,128)(2,1)S(1)}, u32[]{:S(2)}, u32[]{:S(2)}) async-start(bf16[8,4,3584]{2,1,0:T(4,128)(2,1)} %copy.21), calls=%async_computation.2 | async-start | bytes 458752 | tf_op jit(solution)/shard_map/all_to_all | solution.py:98
  31.4 0.7 slice_bitcast_fusion
  32.1 7.2 %all-to-all-done.2 = bf16[8,4,3584]{2,1,0:T(4,128)(2,1)S(1)} async-done(((bf16[8,4,3584]{2,1,0:T(4,128)(2,1)}), bf16[8,4,3584]{2,1,0:T(4,128)(2,1)S(1)}, u32[]{:S(2)}, u32[]{:S(2)}) %all-to-all-start.2) | async-done | bytes 229408 | tf_op jit(solution)/shard_map/all_to_all | solution.py:98
  39.4 0.1 reshape.85
  39.4 2.8 %fusion.63 = f32[32,512]{1,0:T(8,128)S(1)} fusion(bf16[32,3584]{1,0:T(8,128)(2,1)S(1)} %reshape.85, bf16[3584,512]{1,0:T(8,128)(2,1)} %param.13), kind=kOutput, calls=%fused_computation.100 | convolution fusion | flops 117440512 | bytes 3964928 | tf_op jit(solution)/shard_map/dot_general | solution.py:15
  42.2 0.0 copy-start.1
  42.2 4.6 %convolution_convert_fusion.2 = bf16[32,3584]{1,0:T(8,128)(2,1)S(1)} fusion(bf16[512,3584]{1,0:T(8,128)(2,1)} %param.15, bf16[32,3584]{1,0:T(8,128)(2,1)S(1)} %reshape.85, bf16[3584,512]{1,0:T(8,128)(2,1)} %param.14, f32[32,512]{1,0:T(8,128)S(1)} %fusion.63), kind=kOutput, calls=%fused_computation.2 | convolution fusion | flops 235094016 | bytes 7864320 | tf_op jit(solution)/shard_map/dot_general | solution.py:18
  46.8 0.7 convert_element_type.131
  47.6 3.4 %all-to-all-start.3 = ((bf16[8,4,3584]{2,1,0:T(4,128)(2,1)}), bf16[8,4,3584]{2,1,0:T(4,128)(2,1)S(1)}, u32[]{:S(2)}, u32[]{:S(2)}) async-start(bf16[8,4,3584]{2,1,0:T(4,128)(2,1)} %convert_element_type.131), calls=%async_computation.3 | async-start | bytes 458752 | tf_op jit(solution)/shard_map/all_to_all | solution.py:103
  51.0 0.1 fusion.31
  51.1 0.1 select_reduce_fusion.1
  51.2 7.7 %all-to-all-done.3 = bf16[8,4,3584]{2,1,0:T(4,128)(2,1)S(1)} async-done(((bf16[8,4,3584]{2,1,0:T(4,128)(2,1)}), bf16[8,4,3584]{2,1,0:T(4,128)(2,1)S(1)}, u32[]{:S(2)}, u32[]{:S(2)}) %all-to-all-start.3) | async-done | bytes 229408 | tf_op jit(solution)/shard_map/all_to_all | solution.py:103
  58.9 0.3 fusion
  59.2 3.4 %psum.14 = bf16[4,3584]{1,0:T(4,128)(2,1)S(1)} all-reduce(bf16[4,3584]{1,0:T(4,128)(2,1)S(1)} %fusion), channel_id=1, replica_groups=mesh['grp'=2,'ex'=8,'tp'=2] {'tp'}, use_global_device_ids=true, to_apply=%region_6.7 | all-reduce | flops 14336 | bytes 57344 | tf_op jit(solution)/shard_map/psum | solution.py:110
  62.6 0.1 fusion.17
  62.8 0.0 copy-done.1
  62.8 0.3 convolution_convert_fusion.1
  63.1 0.1 copy.23
  63.2 11.6 %all_to_all.31 = bf16[8,4,3584]{2,1,0:T(4,128)(2,1)S(1)} all-to-all(bf16[8,4,3584]{2,1,0:T(4,128)(2,1)S(1)} %copy.23), channel_id=1, replica_groups=mesh['grp'=2,'ex'=8,'tp'=2] {'ex'}, dimensions={0} | all-to-all | bytes 458752 | tf_op jit(solution)/shard_map/all_to_all | solution.py:98
  74.8 0.1 reshape.86
  74.9 2.8 %fusion.64 = f32[32,512]{1,0:T(8,128)S(1)} fusion(bf16[32,3584]{1,0:T(8,128)(2,1)S(1)} %reshape.86, bf16[3584,512]{1,0:T(8,128)(2,1)} %param.13), kind=kOutput, calls=%fused_computation.101 | convolution fusion | flops 117440512 | bytes 3964928 | tf_op jit(solution)/shard_map/dot_general | solution.py:15
  77.7 4.6 %convolution_convert_fusion = bf16[32,3584]{1,0:T(8,128)(2,1)S(1)} fusion(bf16[512,3584]{1,0:T(8,128)(2,1)} %param.15, bf16[32,3584]{1,0:T(8,128)(2,1)S(1)} %reshape.86, bf16[3584,512]{1,0:T(8,128)(2,1)} %param.14, f32[32,512]{1,0:T(8,128)S(1)} %fusion.64), kind=kOutput, calls=%fused_computation | convolution fusion | flops 235094016 | bytes 7864320 | tf_op jit(solution)/shard_map/dot_general | solution.py:18
  82.3 0.7 convert_element_type.142
  83.0 3.4 %all-to-all-start.5 = ((bf16[8,4,3584]{2,1,0:T(4,128)(2,1)}), bf16[8,4,3584]{2,1,0:T(4,128)(2,1)S(1)}, u32[]{:S(2)}, u32[]{:S(2)}) async-start(bf16[8,4,3584]{2,1,0:T(4,128)(2,1)} %convert_element_type.142), calls=%async_computation.5 | async-start | bytes 458752 | tf_op jit(solution)/shard_map/all_to_all | solution.py:103
  86.4 0.1 select_reduce_fusion
  86.5 8.4 %all-to-all-done.5 = bf16[8,4,3584]{2,1,0:T(4,128)(2,1)S(1)} async-done(((bf16[8,4,3584]{2,1,0:T(4,128)(2,1)}), bf16[8,4,3584]{2,1,0:T(4,128)(2,1)S(1)}, u32[]{:S(2)}, u32[]{:S(2)}) %all-to-all-start.5) | async-done | bytes 229408 | tf_op jit(solution)/shard_map/all_to_all | solution.py:103
  94.9 0.3 fusion.1
  95.3 3.4 %psum.15 = bf16[4,3584]{1,0:T(4,128)(2,1)S(1)} all-reduce(bf16[4,3584]{1,0:T(4,128)(2,1)S(1)} %fusion.1), channel_id=1, replica_groups=mesh['grp'=2,'ex'=8,'tp'=2] {'tp'}, use_global_device_ids=true, to_apply=%region_11.12 | all-reduce | flops 14336 | bytes 57344 | tf_op jit(solution)/shard_map/psum | solution.py:110
  98.7 0.6 fusion.20
  (13 shorter events, 0.2 us)
Async XLA Ops:
  0.0 8.9 %copy-start = (bf16[4,3584]{1,0:T(4,128)(2,1)S(1)}, bf16[4,3584]{1,0:T(4,128)(2,1)}, u32[]{:S(2)}) copy-start(bf16[4,3584]{1,0:T(4,128)(2,1)} %param.8) | copy-start | bytes 86020
  1.7 13.6 %all-to-all-start = ((bf16[8,1,2]{2,1,0:T(2,128)(2,1)}), bf16[8,1,2]{2,1,0:T(2,128)(2,1)S(1)}, u32[]{:S(2)}, u32[]{:S(2)}) async-start(bf16[8,1,2]{2,1,0:T(2,128)(2,1)} %convert_element_type.147), calls=%async_computation | async-start | bytes 8192 | tf_op jit(solution)/shard_map/all_to_all | solution.py:62
  15.3 10.5 %all-to-all-start.1 = ((bf16[8,2,3584]{2,1,0:T(2,128)(2,1)}), bf16[8,2,3584]{2,1,0:T(2,128)(2,1)S(1)}, u32[]{:S(2)}, u32[]{:S(2)}) async-start(bf16[8,2,3584]{2,1,0:T(2,128)(2,1)} %reshape.83), calls=%async_computation.1 | async-start | bytes 229376 | tf_op jit(solution)/shard_map/all_to_all | solution.py:61
  28.0 11.3 %all-to-all-start.2 = ((bf16[8,4,3584]{2,1,0:T(4,128)(2,1)}), bf16[8,4,3584]{2,1,0:T(4,128)(2,1)S(1)}, u32[]{:S(2)}, u32[]{:S(2)}) async-start(bf16[8,4,3584]{2,1,0:T(4,128)(2,1)} %copy.21), calls=%async_computation.2 | async-start | bytes 458752 | tf_op jit(solution)/shard_map/all_to_all | solution.py:98
  42.2 20.6 %copy-start.1 = (f32[3584]{0:T(1024)S(1)}, f32[3584]{0:T(1024)}, u32[]{:S(2)}) copy-start(f32[3584]{0:T(1024)} %param.12) | copy-start | bytes 43012
  47.6 11.3 %all-to-all-start.3 = ((bf16[8,4,3584]{2,1,0:T(4,128)(2,1)}), bf16[8,4,3584]{2,1,0:T(4,128)(2,1)S(1)}, u32[]{:S(2)}, u32[]{:S(2)}) async-start(bf16[8,4,3584]{2,1,0:T(4,128)(2,1)} %convert_element_type.131), calls=%async_computation.3 | async-start | bytes 458752 | tf_op jit(solution)/shard_map/all_to_all | solution.py:103
  83.0 11.9 %all-to-all-start.5 = ((bf16[8,4,3584]{2,1,0:T(4,128)(2,1)}), bf16[8,4,3584]{2,1,0:T(4,128)(2,1)S(1)}, u32[]{:S(2)}, u32[]{:S(2)}) async-start(bf16[8,4,3584]{2,1,0:T(4,128)(2,1)} %convert_element_type.142), calls=%async_computation.5 | async-start | bytes 458752 | tf_op jit(solution)/shard_map/all_to_all | solution.py:103
where the time goes:
time: 100 us; the launch traced here: 99.3 us
  waiting for transfers between devices  35 us (35%)
  starting transfers between devices  20.8 us (21%)
  blocking collectives  18.4 us (18%)
  matrix products  17.3 us (17%)
  local copies, waits for them, and re-layouts  5.42 us (5%)
  other arithmetic  2.24 us (2%)
    all_to_all x2, waiting for transfers between devices, shards(): lax.all_to_all(partial_value.reshape(ex_size, slot_cap, features).astype(...  16.1 us
    all_to_all x1, blocking collectives, shards(): lax.all_to_all(packed, 'ex', split_axis=0, concat_axis=0, tiled=True)  11.6 us
    dot_general x2, matrix products, expert_block(): return jnp.dot(activated, w_down, preferred_element_type=jnp.float32)  9.21 us
    all_to_all x1, starting transfers between devices, shards(): lax.all_to_all(labels, 'ex', split_axis=0, concat_axis=0, tiled=True)  7.25 us
    all_to_all x1, waiting for transfers between devices, shards(): lax.all_to_all(packed, 'ex', split_axis=0, concat_axis=0, tiled=True)  7.23 us
    all_to_all x1, waiting for transfers between devices, shards(): lax.all_to_all(outgoing, 'ex', split_axis=0, concat_axis=0, tiled=True)  7.06 us
    all_to_all x2, starting transfers between devices, shards(): lax.all_to_all(partial_value.reshape(ex_size, slot_cap, features).astype(...  6.8 us
    psum x2, blocking collectives, shards(): lax.psum(fold_back(returned, seating, route_coef, experts, group_size).as...  6.8 us
  transfers between devices with their start and end apart: 5, of which 5 were waited for; matrix products, arithmetic and copies ran while one was open for 3% of the time, Pallas kernels for 0%

commit v1 on v0

--- a/solution.py
+++ b/solution.py
@@ -1,6 +1,10 @@
+import functools
+
 import jax
 import jax.numpy as jnp
 from jax import lax
+from jax.experimental import pallas as pl
+from jax.experimental.pallas import tpu as pltpu
 from jax.sharding import PartitionSpec as P
 
 HID = 1024
@@ -114,16 +118,375 @@
     return current
 
 
+QUARTERS = 4
+PIECE = 512
+MESH = pl.DeviceIdType.MESH
+
+
+def one_hot(condition, dtype=jnp.bfloat16):
+    return jnp.where(condition, 1.0, 0.0).astype(dtype)
+
+
+def fused_kernel(
+    n,
+    hidden_ref,
+    place_ref,
+    ids_ref,
+    weights_ref,
+    gain_ref,
+    wg_hbm,
+    wu_hbm,
+    wd_hbm,
+    out_ref,
+    wg,
+    wu,
+    wd,
+    first,
+    second,
+    normed,
+    swap_out,
+    swap_in,
+    stage,
+    parts_out,
+    parts_in,
+    coef,
+    last,
+    weight_sem,
+    gather_send,
+    gather_recv,
+    pass_send,
+    pass_recv,
+    swap_send,
+    swap_recv,
+    back_send,
+    back_recv,
+    last_send,
+    last_recv,
+):
+    rows, features = hidden_ref.shape
+    half = features // 2
+    block = QUARTERS * rows
+    total = n * rows
+    widths = [min(PIECE, half - q * PIECE) for q in range(QUARTERS)]
+    grp, me, core = lax.axis_index("grp"), lax.axis_index("ex"), lax.axis_index("tp")
+    other = 1 - core
+
+    weight_copies = []
+    for h in range(2):
+        span = pl.ds(h * half, half)
+        for which, (source, target) in enumerate(
+            (
+                (wg_hbm.at[span, :], wg.at[span, :]),
+                (wu_hbm.at[span, :], wu.at[span, :]),
+                (wd_hbm.at[:, span], wd.at[h]),
+            )
+        ):
+            weight_copies.append(
+                (which, pltpu.make_async_copy(source, target, weight_sem.at[h * 3 + which]))
+            )
+    for which, copy in sorted(weight_copies, key=lambda pair: pair[0]):
+        copy.start()
+
+    barrier = pltpu.get_barrier_semaphore()
+    for off in range(1, n):
+        pl.semaphore_signal(
+            barrier, inc=1, device_id=(grp, lax.rem(me + off, n), core), device_id_type=MESH
+        )
+    pl.semaphore_signal(barrier, inc=1, device_id=(grp, me, other), device_id_type=MESH)
+
+    mine = pl.ds(pl.multiple_of(me * block, block), block)
+    stage[...] = jnp.zeros_like(stage)
+    held = hidden_ref[...].astype(jnp.float32)
+    for h in range(2):
+        for q in range(QUARTERS):
+            start = h * half + q * PIECE
+            stage[pl.ds(h * block + q * rows, rows), pl.ds(0, widths[q])] = held[
+                :, start : start + widths[q]
+            ]
+    line = lax.broadcasted_iota(jnp.int32, (block, QUARTERS * total), 0)
+    lane = lax.broadcasted_iota(jnp.int32, (block, QUARTERS * total), 1)
+    place = jnp.zeros_like(line)
+    for r in range(rows):
+        place = jnp.where(line % rows == r, place_ref[r], place)
+    placing = one_hot((line // rows == lane // total) & (lane % total == place))
+    for h in range(2):
+        first[h, mine, pl.ds(0, PIECE)] = stage[pl.ds(h * block, block), :].astype(jnp.bfloat16)
+        first[h, mine, pl.ds(PIECE, QUARTERS * total)] = placing
+
+    pl.semaphore_wait(barrier, n)
+
+    def gather_start(step, buf):
+        sends = []
+        for off in range(1, n):
+            copy = pltpu.make_async_remote_copy(
+                src_ref=buf.at[core, mine, :],
+                dst_ref=buf.at[core, mine, :],
+                send_sem=gather_send.at[step, off],
+                recv_sem=gather_recv.at[step, off],
+                device_id=(grp, lax.rem(me + off, n), core),
+                device_id_type=MESH,
+            )
+            copy.start()
+            sends.append(copy)
+        return sends
+
+    def pass_on(step, buf, off):
+        slot = pl.ds(pl.multiple_of(lax.rem(me + n - off, n) * block, block), block)
+        copy = pltpu.make_async_remote_copy(
+            src_ref=buf.at[core, slot, :],
+            dst_ref=buf.at[core, slot, :],
+            send_sem=pass_send.at[step, off],
+            recv_sem=pass_recv.at[step, off],
+            device_id=(grp, me, other),
+            device_id_type=MESH,
+        )
+        copy.start()
+        return copy
+
+    pending = []
+    sends = gather_start(0, first)
+    pending += sends
+
+    for step in range(STEPS):
+        ids = ids_ref[step]
+        weights = weights_ref[step]
+        for e in range(n):
+            value = jnp.sum(jnp.where(ids == e, weights, 0.0), axis=1, keepdims=True)
+            value = jnp.broadcast_to(value, (rows, 128))
+            for q in range(QUARTERS):
+                coef[step, e, pl.ds(q * rows, rows), :] = value
+    stage[...] = jnp.zeros_like(stage)
+
+    current = None
+    for step in range(STEPS):
+        buf = first if step == 0 else second
+        passes = []
+        if step > 0:
+            passes.append(pass_on(step, buf, 0))
+        for off in range(1, n):
+            sends[off - 1].wait_recv()
+            passes.append(pass_on(step, buf, off))
+        for copy in passes:
+            copy.wait_recv()
+        pending += passes
+
+        if step == 0:
+            pick = jnp.transpose(first[0, :, pl.ds(PIECE, QUARTERS * total)].astype(jnp.float32))
+            pick = pick.astype(jnp.bfloat16)
+        else:
+            to = lax.broadcasted_iota(jnp.int32, (QUARTERS * total, n * block), 0)
+            at = lax.broadcasted_iota(jnp.int32, (QUARTERS * total, n * block), 1)
+            pick = one_hot(
+                (to // total == (at // rows) % QUARTERS)
+                & (to % total == (at // block) * rows + at % rows)
+            )
+        spread = [
+            jnp.dot(pick, buf[h, :, pl.ds(0, PIECE)], preferred_element_type=jnp.float32)
+            for h in range(2)
+        ]
+        squares = jnp.sum(spread[0] * spread[0] + spread[1] * spread[1], axis=1, keepdims=True)
+        square = squares[0:total]
+        for q in range(1, QUARTERS):
+            square = square + squares[q * total : (q + 1) * total]
+        scale = lax.rsqrt(square / features + epsilon)
+        for h in range(2):
+            for q in range(QUARTERS):
+                start = h * half + q * PIECE
+                piece = spread[h][q * total : (q + 1) * total, : widths[q]]
+                gain = gain_ref[:, pl.ds(start, widths[q])]
+                normed[:, pl.ds(start, widths[q])] = (piece * scale * gain).astype(jnp.bfloat16)
+        if step == 0:
+            for which, copy in weight_copies:
+                if which < 2:
+                    copy.wait()
+        gate = jnp.dot(normed[...], wg[...], preferred_element_type=jnp.float32)
+        up = jnp.dot(normed[...], wu[...], preferred_element_type=jnp.float32)
+        act = (gate / (1.0 + jnp.exp(-gate)) * up).astype(jnp.bfloat16)
+        if step == 0:
+            for which, copy in weight_copies:
+                if which == 2:
+                    copy.wait()
+        for q in range(QUARTERS):
+            cols = pl.ds(q * PIECE, widths[q])
+            swap_out[step, :, cols] = jnp.dot(
+                act, wd[other, :, cols], preferred_element_type=jnp.float32
+            ).astype(jnp.bfloat16)
+        swap = pltpu.make_async_remote_copy(
+            src_ref=swap_out.at[step],
+            dst_ref=swap_in.at[step],
+            send_sem=swap_send.at[step],
+            recv_sem=swap_recv.at[step],
+            device_id=(grp, me, other),
+            device_id_type=MESH,
+        )
+        swap.start()
+        own = [
+            jnp.dot(
+                act, wd[core, :, pl.ds(q * PIECE, widths[q])], preferred_element_type=jnp.float32
+            )
+            for q in range(QUARTERS)
+        ]
+        if step == 0:
+            to = lax.broadcasted_iota(jnp.int32, (block, QUARTERS * total), 0)
+            at = lax.broadcasted_iota(jnp.int32, (block, QUARTERS * total), 1)
+            keep = one_hot((to // rows == at // total) & (at % total == me * rows + to % rows))
+            spread_own = jnp.where(core == 0, spread[0], spread[1]).astype(jnp.bfloat16)
+            current = jnp.dot(keep, spread_own, preferred_element_type=jnp.float32)
+        swap.wait_recv()
+        pending.append(swap)
+        for q in range(QUARTERS):
+            cols = pl.ds(q * PIECE, widths[q])
+            value = own[q] + swap_in[step, :, cols].astype(jnp.float32)
+            for p in range(n):
+                stage[pl.ds(p * block + q * rows, rows), pl.ds(0, widths[q])] = value[
+                    p * rows : (p + 1) * rows
+                ]
+        parts_out[step] = stage[...].astype(jnp.bfloat16)
+        backs = []
+        for off in range(1, n):
+            peer = lax.rem(me + off, n)
+            copy = pltpu.make_async_remote_copy(
+                src_ref=parts_out.at[step, pl.ds(pl.multiple_of(peer * block, block), block), :],
+                dst_ref=parts_in.at[step, mine, :],
+                send_sem=back_send.at[step, off],
+                recv_sem=back_recv.at[step, off],
+                device_id=(grp, peer, core),
+                device_id_type=MESH,
+            )
+            copy.start()
+            backs.append(copy)
+        parts_in[step, mine, :] = parts_out[step, mine, :]
+        for copy in backs:
+            copy.wait_recv()
+        pending += backs
+        moe = None
+        for e in range(n):
+            value = parts_in[step, pl.ds(e * block, block), :].astype(jnp.float32)
+            value = value * jnp.concatenate([coef[step, e]] * (PIECE // 128), axis=1)
+            moe = value if moe is None else moe + value
+        result = (current + moe).astype(jnp.bfloat16)
+        current = result.astype(jnp.float32)
+        if step < STEPS - 1:
+            second[core, mine, :] = result
+            sends = gather_start(step + 1, second)
+            pending += sends
+
+    last[core] = result
+    final = pltpu.make_async_remote_copy(
+        src_ref=last.at[core],
+        dst_ref=last.at[core],
+        send_sem=last_send,
+        recv_sem=last_recv,
+        device_id=(grp, me, other),
+        device_id_type=MESH,
+    )
+    final.start()
+    final.wait_recv()
+    pending.append(final)
+    for h in range(2):
+        value = last[h].astype(jnp.float32)
+        for q in range(QUARTERS):
+            out_ref[:, pl.ds(h * half + q * PIECE, widths[q])] = value[
+                q * rows : (q + 1) * rows, : widths[q]
+            ].astype(jnp.bfloat16)
+    for copy in pending:
+        copy.wait_send()
+
+
+def fused_shards(hidden_states, draft_row, expert_ids, route_weights, norm_gain, w_gate, w_up, w_down):
+    rows, features = hidden_states.shape
+    hid_dev = w_gate.shape[1]
+    n = lax.axis_size("ex")
+    block = QUARTERS * rows
+    half = features // 2
+    spread = QUARTERS * n * rows
+    vmem, any_space = pl.BlockSpec(memory_space=pltpu.VMEM), pl.BlockSpec(memory_space=pl.ANY)
+    dma = pltpu.SemaphoreType.DMA
+    return pl.pallas_call(
+        functools.partial(fused_kernel, n),
+        out_shape=jax.ShapeDtypeStruct((rows, features), jnp.bfloat16),
+        in_specs=[vmem, pl.BlockSpec(memory_space=pltpu.SMEM), vmem, vmem, vmem]
+        + [any_space] * 3,
+        out_specs=vmem,
+        scratch_shapes=[
+            pltpu.VMEM((features, hid_dev), jnp.bfloat16),
+            pltpu.VMEM((features, hid_dev), jnp.bfloat16),
+            pltpu.VMEM((2, hid_dev, half), jnp.bfloat16),
+            pltpu.VMEM((2, n * block, PIECE + spread), jnp.bfloat16),
+            pltpu.VMEM((2, n * block, PIECE), jnp.bfloat16),
+            pltpu.VMEM((n * rows, features), jnp.bfloat16),
+            pltpu.VMEM((STEPS, n * rows, half), jnp.bfloat16),
+            pltpu.VMEM((STEPS, n * rows, half), jnp.bfloat16),
+            pltpu.VMEM((n * block, PIECE), jnp.float32),
+            pltpu.VMEM((STEPS, n * block, PIECE), jnp.bfloat16),
+            pltpu.VMEM((STEPS, n * block, PIECE), jnp.bfloat16),
+            pltpu.VMEM((STEPS, n, block, 128), jnp.float32),
+            pltpu.VMEM((2, block, PIECE), jnp.bfloat16),
+            dma((6,)),
+            dma((STEPS, n)),
+            dma((STEPS, n)),
+            dma((STEPS, n)),
+            dma((STEPS, n)),
+            dma((STEPS,)),
+            dma((STEPS,)),
+            dma((STEPS, n)),
+            dma((STEPS, n)),
+            dma,
+            dma,
+        ],
+        compiler_params=pltpu.CompilerParams(
+            collective_id=0, has_side_effects=True, vmem_limit_bytes=48 * 1024 * 1024
+        ),
+        cost_estimate=pl.CostEstimate(
+            flops=STEPS * 6 * n * rows * features * hid_dev,
+            bytes_accessed=6 * features * hid_dev,
+            transcendentals=STEPS * n * rows * hid_dev,
+        ),
+    )(
+        hidden_states,
+        draft_row,
+        expert_ids,
+        route_weights,
+        norm_gain.reshape(1, features),
+        w_gate,
+        w_up,
+        w_down,
+    )
+
+
+def by_size(mesh):
+    def run(hidden_states, draft_row, expert_ids, route_weights, norm_gain, w_gate, w_up, w_down):
+        ex = mesh.shape["ex"]
+        rows = hidden_states.shape[0] // (ex * mesh.shape["grp"])
+        every = expert_ids.shape[2] * HID == w_gate.shape[1]
+        one_each = w_gate.shape[1] == ex * HID
+        features = hidden_states.shape[1]
+        shaped = (
+            rows * QUARTERS == 16
+            and features % 256 == 0
+            and (QUARTERS - 1) * PIECE < features // 2 <= QUARTERS * PIECE
+        )
+        dense = every and one_each and shaped and mesh.shape["tp"] == 2
+        in_specs = (
+            P(("grp", "ex"), None),
+            P(("grp", "ex")),
+            P(None, ("grp", "ex"), None),
+            P(None, ("grp", "ex"), None),
+            P(),
+            P(None, ("ex", "tp")),
+            P(None, ("ex", "tp")),
+            P(("ex", "tp"), None),
+        )
+        return jax.shard_map(
+            fused_shards if dense else shards,
+            mesh=mesh,
+            in_specs=in_specs,
+            out_specs=P(("grp", "ex"), None),
+            check_vma=False,
+        )(hidden_states, draft_row, expert_ids, route_weights, norm_gain, w_gate, w_up, w_down)
+
+    return run
+
+
 def solution(mesh):
-    in_specs = (
-        P(("grp", "ex"), None),
-        P(("grp", "ex")),
-        P(None, ("grp", "ex"), None),
-        P(None, ("grp", "ex"), None),
-        P(),
-        P(None, ("ex", "tp")),
-        P(None, ("ex", "tp")),
-        P(("ex", "tp"), None),
-    )
-    out_specs = P(("grp", "ex"), None)
-    return jax.shard_map(shards, mesh=mesh, in_specs=in_specs, out_specs=out_specs, check_vma=False)
+    return by_size(mesh)

time: 100 us -> 43.3 us (0.43)
  Pallas kernels: 0 us -> 36.8 us
  waiting for transfers between devices: 35 us -> 0 us
  starting transfers between devices: 20.8 us -> 0 us
  blocking collectives: 18.4 us -> 0 us
  matrix products: 17.3 us -> 0 us
  other arithmetic: 2.24 us -> 0 us
    pallas_call x0 -> x1, Pallas kernels: none -> 36.8 us  [fused_shards(): pl.pallas_call(functools.partial(fused_kernel, n), out_shape=jax.ShapeDty...]
    all_to_all x5 -> x0, waiting for transfers between devices: 35 us -> none  [the longest x2 16.1 us: shards(): lax.all_to_all(partial_value.reshape(ex_size, slot_cap, features).astype(...]
    all_to_all x5 -> x0, starting transfers between devices: 20.8 us -> none  [the longest x1 7.25 us: shards(): lax.all_to_all(labels, 'ex', split_axis=0, concat_axis=0, tiled=True)]
    dot_general x10 -> x0, matrix products: 17.3 us -> none  [the longest x2 9.21 us: expert_block(): return jnp.dot(activated, w_down, preferred_element_type=jnp.float32)]
    all_to_all x1 -> x0, blocking collectives: 11.6 us -> none  [shards(): lax.all_to_all(packed, 'ex', split_axis=0, concat_axis=0, tiled=True)]
    psum x2 -> x0, blocking collectives: 6.8 us -> none  [shards(): lax.psum(fold_back(returned, seating, route_coef, experts, group_size).as...]
    unnamed x4 -> x11, local copies, waits for them, and re-layouts: 0.01 us -> 5.42 us
    convert_element_type x6 -> x0, local copies, waits for them, and re-layouts: 3.16 us -> none  [the longest x2 1.48 us: shards(): partial_value.reshape(ex_size, slot_cap, features).astype(jnp.bfloat16)]
  transfers between devices with their start and end apart: 5 -> 0, of which waited for: 5 -> 0; matrix products, arithmetic and copies ran while one was open for 3% -> 0% of each run, Pallas kernels for 0% -> 0%
where the time goes in v1:
time: 43.3 us; the launch traced here: 43 us
  Pallas kernels  36.8 us (85%)
  local copies, waits for them, and re-layouts  6.15 us (14%)
    pallas_call x1, Pallas kernels, fused_shards(): pl.pallas_call(functools.partial(fused_kernel, n), out_shape=jax.ShapeDty...  36.8 us
    unnamed x11, local copies, waits for them, and re-layouts  5.42 us

profile of v1, /device:TPU:0, one launch (start us, length us, event | category | flops | bytes accessed | tf_op | source)
XLA Modules:
  0.0 43.0 jit_solution(17069198174828539317)
XLA Ops:
  0.0 0.7 %reshape.3.gain_ref = f32[1,3584]{1,0:T(1,128)S(1)} reshape(f32[3584]{0:T(1024)} %param.12) | data formatting | bytes 28672 | tf_op jit(solution)/shard_map/reshape | solution.py:450
  0.7 0.0 copy-start
  0.7 2.0 %copy-done = bf16[3584,512]{1,0:T(8,128)(2,1)S(1)} copy-done((bf16[3584,512]{1,0:T(8,128)(2,1)S(1)}, bf16[3584,512]{1,0:T(8,128)(2,1)}, u32[]{:S(2)}) %copy-start) | copy-done | bytes 3670040
  2.8 0.0 copy-start.1
  2.8 0.7 %copy-done.1 = bf16[4,3584]{1,0:T(4,128)(2,1)S(1)} copy-done((bf16[4,3584]{1,0:T(4,128)(2,1)S(1)}, bf16[4,3584]{1,0:T(4,128)(2,1)}, u32[]{:S(2)}) %copy-start.1) | copy-done | bytes 28696
  3.5 0.0 copy-start.2
  3.5 0.7 %copy-done.2 = s32[2,4,8]{2,1,0:T(4,128)S(1)} copy-done((s32[2,4,8]{2,1,0:T(4,128)S(1)}, s32[2,4,8]{2,1,0:T(4,128)}, u32[]{:S(2)}) %copy-start.2) | copy-done | bytes 280
  4.2 0.0 copy-start.3
  4.2 0.7 %copy-done.3 = f32[2,4,8]{2,1,0:T(4,128)S(1)} copy-done((f32[2,4,8]{2,1,0:T(4,128)S(1)}, f32[2,4,8]{2,1,0:T(4,128)}, u32[]{:S(2)}) %copy-start.3) | copy-done | bytes 280
  4.9 0.0 copy-start.4
  4.9 0.7 %copy-done.4 = s32[4]{0:T(128)S(1)} copy-done((s32[4]{0:T(128)S(1)}, s32[4]{0:T(128)}, u32[]{:S(2)}) %copy-start.4) | copy-done | bytes 40
  5.6 36.8 %shard_map.82 = bf16[4,3584]{1,0:T(4,128)(2,1)S(1)} custom-call(bf16[4,3584]{1,0:T(4,128)(2,1)S(1)} %copy-done.1, s32[4]{0:T(128)S(1)} %copy-done.4, s32[2,4,8]{2,1,0:T(4,128)S(1)} %copy-done.2, f32[2,4,8]{2,1,0:T(4,128)S(1)} %copy-done.3, f32[1,3584]{1,0:T(1,128)S(1)} %reshape.3.gain_ref, bf16[3584,512]{1,0:T(8,128)(2,1)S(1)} %copy-done, ...), custom_call_target="tpu_custom_call" | custom-call | flops 704643072 | bytes 11010048 | tf_op jit(solution)/shard_map/pallas_call | solution.py:405
  42.4 0.6 %copy.10 = bf16[4,3584]{1,0:T(4,128)(2,1)} copy(bf16[4,3584]{1,0:T(4,128)(2,1)S(1)} %shard_map.82) | data formatting | bytes 57344
Async XLA Ops:
  0.7 2.0 %copy-start = (bf16[3584,512]{1,0:T(8,128)(2,1)S(1)}, bf16[3584,512]{1,0:T(8,128)(2,1)}, u32[]{:S(2)}) copy-start(bf16[3584,512]{1,0:T(8,128)(2,1)} %wg_hbm.1) | copy-start | bytes 11010052
  2.8 0.7 %copy-start.1 = (bf16[4,3584]{1,0:T(4,128)(2,1)S(1)}, bf16[4,3584]{1,0:T(4,128)(2,1)}, u32[]{:S(2)}) copy-start(bf16[4,3584]{1,0:T(4,128)(2,1)} %hidden_ref.1) | copy-start | bytes 86020
  3.5 0.7 %copy-start.2 = (s32[2,4,8]{2,1,0:T(4,128)S(1)}, s32[2,4,8]{2,1,0:T(4,128)}, u32[]{:S(2)}) copy-start(s32[2,4,8]{2,1,0:T(4,128)} %ids_ref.1) | copy-start | bytes 772
  4.2 0.7 %copy-start.3 = (f32[2,4,8]{2,1,0:T(4,128)S(1)}, f32[2,4,8]{2,1,0:T(4,128)}, u32[]{:S(2)}) copy-start(f32[2,4,8]{2,1,0:T(4,128)} %weights_ref.1) | copy-start | bytes 772
  4.9 0.7 %copy-start.4 = (s32[4]{0:T(128)S(1)}, s32[4]{0:T(128)}, u32[]{:S(2)}) copy-start(s32[4]{0:T(128)} %place_ref.1) | copy-start | bytes 52

commit v2 on v1

--- a/solution.py
+++ b/solution.py
@@ -129,15 +129,20 @@
 
 def fused_kernel(
     n,
+    hidden_hbm,
+    place_hbm,
+    ids_hbm,
+    weights_hbm,
+    gain_hbm,
+    wg_hbm,
+    wu_hbm,
+    wd_hbm,
+    out_ref,
     hidden_ref,
     place_ref,
     ids_ref,
     weights_ref,
     gain_ref,
-    wg_hbm,
-    wu_hbm,
-    wd_hbm,
-    out_ref,
     wg,
     wu,
     wd,
@@ -151,6 +156,7 @@
     parts_in,
     coef,
     last,
+    small_sem,
     weight_sem,
     gather_send,
     gather_recv,
@@ -171,6 +177,20 @@
     grp, me, core = lax.axis_index("grp"), lax.axis_index("ex"), lax.axis_index("tp")
     other = 1 - core
 
+    small = [
+        pltpu.make_async_copy(source, target, small_sem.at[i])
+        for i, (source, target) in enumerate(
+            (
+                (hidden_hbm, hidden_ref),
+                (place_hbm, place_ref),
+                (ids_hbm, ids_ref),
+                (weights_hbm, weights_ref),
+                (gain_hbm, gain_ref),
+            )
+        )
+    ]
+    for copy in small:
+        copy.start()
     weight_copies = []
     for h in range(2):
         span = pl.ds(h * half, half)
@@ -196,6 +216,8 @@
 
     mine = pl.ds(pl.multiple_of(me * block, block), block)
     stage[...] = jnp.zeros_like(stage)
+    for copy in small:
+        copy.wait()
     held = hidden_ref[...].astype(jnp.float32)
     for h in range(2):
         for q in range(QUARTERS):
@@ -293,7 +315,7 @@
             for q in range(QUARTERS):
                 start = h * half + q * PIECE
                 piece = spread[h][q * total : (q + 1) * total, : widths[q]]
-                gain = gain_ref[:, pl.ds(start, widths[q])]
+                gain = gain_ref[pl.ds(start, widths[q])].reshape(1, widths[q])
                 normed[:, pl.ds(start, widths[q])] = (piece * scale * gain).astype(jnp.bfloat16)
         if step == 0:
             for which, copy in weight_copies:
@@ -400,15 +422,19 @@
     block = QUARTERS * rows
     half = features // 2
     spread = QUARTERS * n * rows
-    vmem, any_space = pl.BlockSpec(memory_space=pltpu.VMEM), pl.BlockSpec(memory_space=pl.ANY)
+    vmem, hbm = pl.BlockSpec(memory_space=pltpu.VMEM), pl.BlockSpec(memory_space=pltpu.HBM)
     dma = pltpu.SemaphoreType.DMA
     return pl.pallas_call(
         functools.partial(fused_kernel, n),
         out_shape=jax.ShapeDtypeStruct((rows, features), jnp.bfloat16),
-        in_specs=[vmem, pl.BlockSpec(memory_space=pltpu.SMEM), vmem, vmem, vmem]
-        + [any_space] * 3,
+        in_specs=[hbm] * 8,
         out_specs=vmem,
         scratch_shapes=[
+            pltpu.VMEM((rows, features), jnp.bfloat16),
+            pltpu.SMEM((rows,), jnp.int32),
+            pltpu.VMEM(expert_ids.shape, jnp.int32),
+            pltpu.VMEM(route_weights.shape, jnp.float32),
+            pltpu.VMEM((features,), jnp.float32),
             pltpu.VMEM((features, hid_dev), jnp.bfloat16),
             pltpu.VMEM((features, hid_dev), jnp.bfloat16),
             pltpu.VMEM((2, hid_dev, half), jnp.bfloat16),
@@ -422,6 +448,7 @@
             pltpu.VMEM((STEPS, n * block, PIECE), jnp.bfloat16),
             pltpu.VMEM((STEPS, n, block, 128), jnp.float32),
             pltpu.VMEM((2, block, PIECE), jnp.bfloat16),
+            dma((5,)),
             dma((6,)),
             dma((STEPS, n)),
             dma((STEPS, n)),
@@ -435,7 +462,7 @@
             dma,
         ],
         compiler_params=pltpu.CompilerParams(
-            collective_id=0, has_side_effects=True, vmem_limit_bytes=48 * 1024 * 1024
+            collective_id=0, has_side_effects=True, vmem_limit_bytes=63 * 1024 * 1024
         ),
         cost_estimate=pl.CostEstimate(
             flops=STEPS * 6 * n * rows * features * hid_dev,
@@ -447,7 +474,7 @@
         draft_row,
         expert_ids,
         route_weights,
-        norm_gain.reshape(1, features),
+        norm_gain,
         w_gate,
         w_up,
         w_down,

time: 43.3 us -> 38.5 us (0.89)
  local copies, waits for them, and re-layouts: 6.15 us -> 1.37 us
    unnamed x11 -> x1, local copies, waits for them, and re-layouts: 5.42 us -> 1.37 us
    reshape x1 -> x0, local copies, waits for them, and re-layouts: 0.73 us -> none  [fused_shards(): norm_gain.reshape(1, features)]
where the time goes in v2:
time: 38.5 us; the launch traced here: 38.3 us
  Pallas kernels  36.9 us (96%)
  local copies, waits for them, and re-layouts  1.37 us (4%)
    pallas_call x1, Pallas kernels, fused_shards(): pl.pallas_call(functools.partial(fused_kernel, n), out_shape=jax.ShapeDty...  36.9 us
    unnamed x1, local copies, waits for them, and re-layouts  1.37 us

profile of v2, /device:TPU:0, one launch (start us, length us, event | category | flops | bytes accessed | tf_op | source)
XLA Modules:
  0.0 38.3 jit_solution(7320624317804049828)
XLA Ops:
  0.0 36.9 %shard_map.82 = bf16[4,3584]{1,0:T(4,128)(2,1)} custom-call(bf16[4,3584]{1,0:T(4,128)(2,1)} %hidden_hbm.1, s32[4]{0:T(128)} %place_hbm.1, s32[2,4,8]{2,1,0:T(4,128)} %ids_hbm.1, f32[2,4,8]{2,1,0:T(4,128)} %weights_hbm.1, f32[3584]{0:T(1024)} %gain_hbm.1, bf16[3584,512]{1,0:T(8,128)(2,1)} %wg_hbm.1, bf16[3584,512]{1,0:T(8,128)(2,1)} %wu_hbm.1, ...), custom_call_target="tpu_custom_call" | custom-call | flops 704643072 | bytes 11010048 | tf_op jit(solution)/shard_map/pallas_call | solution.py:427
  36.9 1.4 %copy.10 = bf16[4,3584]{1,0:T(4,128)(2,1)} copy(bf16[4,3584]{1,0:T(4,128)(2,1)} %shard_map.82) | data formatting | bytes 57344

commit v3 on v2

--- a/solution.py
+++ b/solution.py
@@ -148,6 +148,7 @@
     wd,
     first,
     second,
+    ordered,
     normed,
     swap_out,
     swap_in,
@@ -196,16 +197,16 @@
         span = pl.ds(h * half, half)
         for which, (source, target) in enumerate(
             (
-                (wg_hbm.at[span, :], wg.at[span, :]),
-                (wu_hbm.at[span, :], wu.at[span, :]),
+                (wg_hbm.at[span, :], wg.at[h]),
+                (wu_hbm.at[span, :], wu.at[h]),
                 (wd_hbm.at[:, span], wd.at[h]),
             )
         ):
             weight_copies.append(
-                (which, pltpu.make_async_copy(source, target, weight_sem.at[h * 3 + which]))
-            )
-    for which, copy in sorted(weight_copies, key=lambda pair: pair[0]):
-        copy.start()
+                pltpu.make_async_copy(source, target, weight_sem.at[h * 3 + which])
+            )
+    for i in (0, 3, 1, 4, 2, 5):
+        weight_copies[i].start()
 
     barrier = pltpu.get_barrier_semaphore()
     for off in range(1, n):
@@ -278,6 +279,33 @@
             for q in range(QUARTERS):
                 coef[step, e, pl.ds(q * rows, rows), :] = value
     stage[...] = jnp.zeros_like(stage)
+    to = lax.broadcasted_iota(jnp.int32, (QUARTERS * total, n * block), 0)
+    at = lax.broadcasted_iota(jnp.int32, (QUARTERS * total, n * block), 1)
+    ordered[...] = one_hot(
+        (to // total == (at // rows) % QUARTERS)
+        & (to % total == (at // block) * rows + at % rows)
+    )
+    for copy in weight_copies[0:2] + weight_copies[3:5]:
+        copy.wait()
+
+    def half_product(buf, h, pick):
+        spread = jnp.dot(pick, buf[h, :, pl.ds(0, PIECE)], preferred_element_type=jnp.float32)
+        squares = jnp.sum(spread * spread, axis=1, keepdims=True)
+        square = squares[0:total]
+        for q in range(1, QUARTERS):
+            square = square + squares[q * total : (q + 1) * total]
+        scale = lax.rsqrt(square / half + epsilon)
+        for q in range(QUARTERS):
+            gains = [
+                gain_ref[pl.ds(side * half + q * PIECE, widths[q])].reshape(1, widths[q])
+                for side in range(2)
+            ]
+            gain = jnp.where(h == 0, gains[0], gains[1])
+            piece = spread[q * total : (q + 1) * total, : widths[q]]
+            normed[h, :, pl.ds(q * PIECE, widths[q])] = (piece * scale * gain).astype(jnp.bfloat16)
+        gate = jnp.dot(normed[h], wg[h], preferred_element_type=jnp.float32)
+        up = jnp.dot(normed[h], wu[h], preferred_element_type=jnp.float32)
+        return spread, square, scale, gate, up
 
     current = None
     for step in range(STEPS):
@@ -288,46 +316,26 @@
         for off in range(1, n):
             sends[off - 1].wait_recv()
             passes.append(pass_on(step, buf, off))
+        pending += passes
+        if step == 0:
+            pick = jnp.transpose(
+                first[core, :, pl.ds(PIECE, QUARTERS * total)].astype(jnp.float32)
+            ).astype(jnp.bfloat16)
+        else:
+            pick = ordered[...]
+        spread_own, square_own, scale_own, gate_own, up_own = half_product(buf, core, pick)
         for copy in passes:
             copy.wait_recv()
-        pending += passes
-
-        if step == 0:
-            pick = jnp.transpose(first[0, :, pl.ds(PIECE, QUARTERS * total)].astype(jnp.float32))
-            pick = pick.astype(jnp.bfloat16)
-        else:
-            to = lax.broadcasted_iota(jnp.int32, (QUARTERS * total, n * block), 0)
-            at = lax.broadcasted_iota(jnp.int32, (QUARTERS * total, n * block), 1)
-            pick = one_hot(
-                (to // total == (at // rows) % QUARTERS)
-                & (to % total == (at // block) * rows + at % rows)
-            )
-        spread = [
-            jnp.dot(pick, buf[h, :, pl.ds(0, PIECE)], preferred_element_type=jnp.float32)
-            for h in range(2)
-        ]
-        squares = jnp.sum(spread[0] * spread[0] + spread[1] * spread[1], axis=1, keepdims=True)
-        square = squares[0:total]
-        for q in range(1, QUARTERS):
-            square = square + squares[q * total : (q + 1) * total]
-        scale = lax.rsqrt(square / features + epsilon)
-        for h in range(2):
-            for q in range(QUARTERS):
-                start = h * half + q * PIECE
-                piece = spread[h][q * total : (q + 1) * total, : widths[q]]
-                gain = gain_ref[pl.ds(start, widths[q])].reshape(1, widths[q])
-                normed[:, pl.ds(start, widths[q])] = (piece * scale * gain).astype(jnp.bfloat16)
-        if step == 0:
-            for which, copy in weight_copies:
-                if which < 2:
-                    copy.wait()
-        gate = jnp.dot(normed[...], wg[...], preferred_element_type=jnp.float32)
-        up = jnp.dot(normed[...], wu[...], preferred_element_type=jnp.float32)
+        _, square_other, scale_other, gate_other, up_other = half_product(buf, other, pick)
+        scale = lax.rsqrt((square_own + square_other) / features + epsilon)
+        fit_own = jnp.where(scale == 0.0, 0.0, scale / scale_own)
+        fit_other = jnp.where(scale == 0.0, 0.0, scale / scale_other)
+        gate = gate_own * fit_own + gate_other * fit_other
+        up = up_own * fit_own + up_other * fit_other
         act = (gate / (1.0 + jnp.exp(-gate)) * up).astype(jnp.bfloat16)
         if step == 0:
-            for which, copy in weight_copies:
-                if which == 2:
-                    copy.wait()
+            for copy in weight_copies[2::3]:
+                copy.wait()
         for q in range(QUARTERS):
             cols = pl.ds(q * PIECE, widths[q])
             swap_out[step, :, cols] = jnp.dot(
@@ -352,8 +360,9 @@
             to = lax.broadcasted_iota(jnp.int32, (block, QUARTERS * total), 0)
             at = lax.broadcasted_iota(jnp.int32, (block, QUARTERS * total), 1)
             keep = one_hot((to // rows == at // total) & (at % total == me * rows + to % rows))
-            spread_own = jnp.where(core == 0, spread[0], spread[1]).astype(jnp.bfloat16)
-            current = jnp.dot(keep, spread_own, preferred_element_type=jnp.float32)
+            current = jnp.dot(
+                keep, spread_own.astype(jnp.bfloat16), preferred_element_type=jnp.float32
+            )
         swap.wait_recv()
         pending.append(swap)
         for q in range(QUARTERS):
@@ -435,12 +444,13 @@
             pltpu.VMEM(expert_ids.shape, jnp.int32),
             pltpu.VMEM(route_weights.shape, jnp.float32),
             pltpu.VMEM((features,), jnp.float32),
-            pltpu.VMEM((features, hid_dev), jnp.bfloat16),
-            pltpu.VMEM((features, hid_dev), jnp.bfloat16),
+            pltpu.VMEM((2, half, hid_dev), jnp.bfloat16),
+            pltpu.VMEM((2, half, hid_dev), jnp.bfloat16),
             pltpu.VMEM((2, hid_dev, half), jnp.bfloat16),
             pltpu.VMEM((2, n * block, PIECE + spread), jnp.bfloat16),
             pltpu.VMEM((2, n * block, PIECE), jnp.bfloat16),
-            pltpu.VMEM((n * rows, features), jnp.bfloat16),
+            pltpu.VMEM((spread, n * block), jnp.bfloat16),
+            pltpu.VMEM((2, n * rows, half), jnp.bfloat16),
             pltpu.VMEM((STEPS, n * rows, half), jnp.bfloat16),
             pltpu.VMEM((STEPS, n * rows, half), jnp.bfloat16),
             pltpu.VMEM((n * block, PIECE), jnp.float32),

time: 38.5 us -> 38.3 us (level)
  no operation moved by 1% of the time
where the time goes in v3:
time: 38.3 us; the launch traced here: 38.1 us
  Pallas kernels  36.7 us (96%)
  local copies, waits for them, and re-layouts  1.37 us (4%)
    pallas_call x1, Pallas kernels, fused_shards(): pl.pallas_call(functools.partial(fused_kernel, n), out_shape=jax.ShapeDty...  36.7 us
    unnamed x1, local copies, waits for them, and re-layouts  1.37 us

profile of v3, /device:TPU:0, one launch (start us, length us, event | category | flops | bytes accessed | tf_op | source)
XLA Modules:
  0.0 38.1 jit_solution(17426044515205807597)
XLA Ops:
  0.0 36.7 %shard_map.82 = bf16[4,3584]{1,0:T(4,128)(2,1)} custom-call(bf16[4,3584]{1,0:T(4,128)(2,1)} %hidden_hbm.1, s32[4]{0:T(128)} %place_hbm.1, s32[2,4,8]{2,1,0:T(4,128)} %ids_hbm.1, f32[2,4,8]{2,1,0:T(4,128)} %weights_hbm.1, f32[3584]{0:T(1024)} %gain_hbm.1, bf16[3584,512]{1,0:T(8,128)(2,1)} %wg_hbm.1, bf16[3584,512]{1,0:T(8,128)(2,1)} %wu_hbm.1, ...), custom_call_target="tpu_custom_call" | custom-call | flops 704643072 | bytes 11010048 | tf_op jit(solution)/shard_map/pallas_call | solution.py:436
  36.7 1.4 %copy.10 = bf16[4,3584]{1,0:T(4,128)(2,1)} copy(bf16[4,3584]{1,0:T(4,128)(2,1)} %shard_map.82) | data formatting | bytes 57344

commit v4 on v3

--- a/solution.py
+++ b/solution.py
@@ -120,6 +120,7 @@
 
 QUARTERS = 4
 PIECE = 512
+CHUNKS = 2
 MESH = pl.DeviceIdType.MESH
 
 
@@ -238,14 +239,14 @@
 
     pl.semaphore_wait(barrier, n)
 
-    def gather_start(step, buf):
+    def gather_start(step, buf, cols, chunk):
         sends = []
         for off in range(1, n):
             copy = pltpu.make_async_remote_copy(
-                src_ref=buf.at[core, mine, :],
-                dst_ref=buf.at[core, mine, :],
-                send_sem=gather_send.at[step, off],
-                recv_sem=gather_recv.at[step, off],
+                src_ref=buf.at[core, mine, cols],
+                dst_ref=buf.at[core, mine, cols],
+                send_sem=gather_send.at[step * CHUNKS + chunk, off],
+                recv_sem=gather_recv.at[step * CHUNKS + chunk, off],
                 device_id=(grp, lax.rem(me + off, n), core),
                 device_id_type=MESH,
             )
@@ -267,8 +268,8 @@
         return copy
 
     pending = []
-    sends = gather_start(0, first)
-    pending += sends
+    sends = [gather_start(0, first, pl.ds(0, PIECE + QUARTERS * total), 0)]
+    pending += sends[0]
 
     for step in range(STEPS):
         ids = ids_ref[step]
@@ -314,7 +315,8 @@
         if step > 0:
             passes.append(pass_on(step, buf, 0))
         for off in range(1, n):
-            sends[off - 1].wait_recv()
+            for chunk in sends:
+                chunk[off - 1].wait_recv()
             passes.append(pass_on(step, buf, off))
         pending += passes
         if step == 0:
@@ -373,34 +375,44 @@
                     p * rows : (p + 1) * rows
                 ]
         parts_out[step] = stage[...].astype(jnp.bfloat16)
+        parts_in[step, mine, :] = parts_out[step, mine, :]
+        width = PIECE // CHUNKS
         backs = []
-        for off in range(1, n):
-            peer = lax.rem(me + off, n)
-            copy = pltpu.make_async_remote_copy(
-                src_ref=parts_out.at[step, pl.ds(pl.multiple_of(peer * block, block), block), :],
-                dst_ref=parts_in.at[step, mine, :],
-                send_sem=back_send.at[step, off],
-                recv_sem=back_recv.at[step, off],
-                device_id=(grp, peer, core),
-                device_id_type=MESH,
-            )
-            copy.start()
-            backs.append(copy)
-        parts_in[step, mine, :] = parts_out[step, mine, :]
-        for copy in backs:
-            copy.wait_recv()
+        for chunk in range(CHUNKS):
+            cols = pl.ds(chunk * width, width)
+            for off in range(1, n):
+                peer = lax.rem(me + off, n)
+                slot = pl.ds(pl.multiple_of(peer * block, block), block)
+                copy = pltpu.make_async_remote_copy(
+                    src_ref=parts_out.at[step, slot, cols],
+                    dst_ref=parts_in.at[step, mine, cols],
+                    send_sem=back_send.at[step * CHUNKS + chunk, off],
+                    recv_sem=back_recv.at[step * CHUNKS + chunk, off],
+                    device_id=(grp, peer, core),
+                    device_id_type=MESH,
+                )
+                copy.start()
+                backs.append(copy)
         pending += backs
-        moe = None
-        for e in range(n):
-            value = parts_in[step, pl.ds(e * block, block), :].astype(jnp.float32)
-            value = value * jnp.concatenate([coef[step, e]] * (PIECE // 128), axis=1)
-            moe = value if moe is None else moe + value
-        result = (current + moe).astype(jnp.bfloat16)
+        results, sends = [], []
+        for chunk in range(CHUNKS):
+            cols = pl.ds(chunk * width, width)
+            for copy in backs[chunk * (n - 1) : (chunk + 1) * (n - 1)]:
+                copy.wait_recv()
+            moe = None
+            for e in range(n):
+                value = parts_in[step, pl.ds(e * block, block), cols].astype(jnp.float32)
+                value = value * jnp.concatenate([coef[step, e]] * (width // 128), axis=1)
+                moe = value if moe is None else moe + value
+            before = current[:, chunk * width : (chunk + 1) * width]
+            piece = (before + moe).astype(jnp.bfloat16)
+            results.append(piece)
+            if step < STEPS - 1:
+                second[core, mine, cols] = piece
+                sends.append(gather_start(step + 1, second, cols, chunk))
+                pending += sends[-1]
+        result = jnp.concatenate(results, axis=1)
         current = result.astype(jnp.float32)
-        if step < STEPS - 1:
-            second[core, mine, :] = result
-            sends = gather_start(step + 1, second)
-            pending += sends
 
     last[core] = result
     final = pltpu.make_async_remote_copy(
@@ -460,14 +472,14 @@
             pltpu.VMEM((2, block, PIECE), jnp.bfloat16),
             dma((5,)),
             dma((6,)),
-            dma((STEPS, n)),
-            dma((STEPS, n)),
+            dma((STEPS * CHUNKS, n)),
+            dma((STEPS * CHUNKS, n)),
             dma((STEPS, n)),
             dma((STEPS, n)),
             dma((STEPS,)),
             dma((STEPS,)),
-            dma((STEPS, n)),
-            dma((STEPS, n)),
+            dma((STEPS * CHUNKS, n)),
+            dma((STEPS * CHUNKS, n)),
             dma,
             dma,
         ],

time: 38.3 us -> 38.9 us (1.016)
  Pallas kernels: 36.7 us -> 37.3 us
    pallas_call x1, Pallas kernels: 36.7 us -> 37.3 us  [fused_shards(): pl.pallas_call(functools.partial(fused_kernel, n), out_shape=jax.ShapeDty...]
where the time goes in v4:
time: 38.9 us; the launch traced here: 38.7 us
  Pallas kernels  37.3 us (96%)
  local copies, waits for them, and re-layouts  1.37 us (4%)
    pallas_call x1, Pallas kernels, fused_shards(): pl.pallas_call(functools.partial(fused_kernel, n), out_shape=jax.ShapeDty...  37.3 us
    unnamed x1, local copies, waits for them, and re-layouts  1.37 us

profile of v4, /device:TPU:0, one launch (start us, length us, event | category | flops | bytes accessed | tf_op | source)
XLA Modules:
  0.0 38.7 jit_solution(7439689467689747560)
XLA Ops:
  0.0 37.3 %shard_map.82 = bf16[4,3584]{1,0:T(4,128)(2,1)} custom-call(bf16[4,3584]{1,0:T(4,128)(2,1)} %hidden_hbm.1, s32[4]{0:T(128)} %place_hbm.1, s32[2,4,8]{2,1,0:T(4,128)} %ids_hbm.1, f32[2,4,8]{2,1,0:T(4,128)} %weights_hbm.1, f32[3584]{0:T(1024)} %gain_hbm.1, bf16[3584,512]{1,0:T(8,128)(2,1)} %wg_hbm.1, bf16[3584,512]{1,0:T(8,128)(2,1)} %wu_hbm.1, ...), custom_call_target="tpu_custom_call" | custom-call | flops 704643072 | bytes 11010048 | tf_op jit(solution)/shard_map/pallas_call | solution.py:448
  37.3 1.4 %copy.10 = bf16[4,3584]{1,0:T(4,128)(2,1)} copy(bf16[4,3584]{1,0:T(4,128)(2,1)} %shard_map.82) | data formatting | bytes 57344

commit v5 on v3

--- a/solution.py
+++ b/solution.py
@@ -178,6 +178,16 @@
     grp, me, core = lax.axis_index("grp"), lax.axis_index("ex"), lax.axis_index("tp")
     other = 1 - core
 
+    def partner(off):
+        index, digit = 0, 1
+        while digit < n:
+            own = lax.rem(me // digit, 2)
+            index = index + (1 - own if off // digit % 2 else own) * digit
+            digit *= 2
+        return index
+
+    turns = sorted(range(1, n), key=lambda off: (off >= n // 2, off % 2, off), reverse=True)
+
     small = [
         pltpu.make_async_copy(source, target, small_sem.at[i])
         for i, (source, target) in enumerate(
@@ -209,9 +219,9 @@
         weight_copies[i].start()
 
     barrier = pltpu.get_barrier_semaphore()
-    for off in range(1, n):
+    for off in turns:
         pl.semaphore_signal(
-            barrier, inc=1, device_id=(grp, lax.rem(me + off, n), core), device_id_type=MESH
+            barrier, inc=1, device_id=(grp, partner(off), core), device_id_type=MESH
         )
     pl.semaphore_signal(barrier, inc=1, device_id=(grp, me, other), device_id_type=MESH)
 
@@ -240,13 +250,13 @@
 
     def gather_start(step, buf):
         sends = []
-        for off in range(1, n):
+        for off in turns:
             copy = pltpu.make_async_remote_copy(
                 src_ref=buf.at[core, mine, :],
                 dst_ref=buf.at[core, mine, :],
                 send_sem=gather_send.at[step, off],
                 recv_sem=gather_recv.at[step, off],
-                device_id=(grp, lax.rem(me + off, n), core),
+                device_id=(grp, partner(off), core),
                 device_id_type=MESH,
             )
             copy.start()
@@ -254,7 +264,7 @@
         return sends
 
     def pass_on(step, buf, off):
-        slot = pl.ds(pl.multiple_of(lax.rem(me + n - off, n) * block, block), block)
+        slot = pl.ds(pl.multiple_of((partner(off) if off else me) * block, block), block)
         copy = pltpu.make_async_remote_copy(
             src_ref=buf.at[core, slot, :],
             dst_ref=buf.at[core, slot, :],
@@ -313,8 +323,8 @@
         passes = []
         if step > 0:
             passes.append(pass_on(step, buf, 0))
-        for off in range(1, n):
-            sends[off - 1].wait_recv()
+        for off in turns:
+            sends[turns.index(off)].wait_recv()
             passes.append(pass_on(step, buf, off))
         pending += passes
         if step == 0:
@@ -374,8 +384,8 @@
                 ]
         parts_out[step] = stage[...].astype(jnp.bfloat16)
         backs = []
-        for off in range(1, n):
-            peer = lax.rem(me + off, n)
+        for off in turns:
+            peer = partner(off)
             copy = pltpu.make_async_remote_copy(
                 src_ref=parts_out.at[step, pl.ds(pl.multiple_of(peer * block, block), block), :],
                 dst_ref=parts_in.at[step, mine, :],
@@ -503,7 +513,8 @@
             and features % 256 == 0
             and (QUARTERS - 1) * PIECE < features // 2 <= QUARTERS * PIECE
         )
-        dense = every and one_each and shaped and mesh.shape["tp"] == 2
+        ex_power = ex & (ex - 1) == 0
+        dense = ex_power and every and one_each and shaped and mesh.shape["tp"] == 2
         in_specs = (
             P(("grp", "ex"), None),
             P(("grp", "ex")),

time: 38.3 us -> 38.6 us (level)
  no operation moved by 1% of the time
where the time goes in v5:
time: 38.6 us; the launch traced here: 38.4 us
  Pallas kernels  37 us (96%)
  local copies, waits for them, and re-layouts  1.37 us (4%)
    pallas_call x1, Pallas kernels, fused_shards(): pl.pallas_call(functools.partial(fused_kernel, n), out_shape=jax.ShapeDty...  37 us
    unnamed x1, local copies, waits for them, and re-layouts  1.37 us

profile of v5, /device:TPU:0, one launch (start us, length us, event | category | flops | bytes accessed | tf_op | source)
XLA Modules:
  0.0 38.4 jit_solution(15365459997472393107)
XLA Ops:
  0.0 37.0 %shard_map.82 = bf16[4,3584]{1,0:T(4,128)(2,1)} custom-call(bf16[4,3584]{1,0:T(4,128)(2,1)} %hidden_hbm.1, s32[4]{0:T(128)} %place_hbm.1, s32[2,4,8]{2,1,0:T(4,128)} %ids_hbm.1, f32[2,4,8]{2,1,0:T(4,128)} %weights_hbm.1, f32[3584]{0:T(1024)} %gain_hbm.1, bf16[3584,512]{1,0:T(8,128)(2,1)} %wg_hbm.1, bf16[3584,512]{1,0:T(8,128)(2,1)} %wu_hbm.1, ...), custom_call_target="tpu_custom_call" | custom-call | flops 704643072 | bytes 11010048 | tf_op jit(solution)/shard_map/pallas_call | solution.py:446
  37.0 1.4 %copy.10 = bf16[4,3584]{1,0:T(4,128)(2,1)} copy(bf16[4,3584]{1,0:T(4,128)(2,1)} %shard_map.82) | data formatting | bytes 57344

commit v6 on v3

--- a/solution.py
+++ b/solution.py
@@ -192,6 +192,13 @@
     ]
     for copy in small:
         copy.start()
+    barrier = pltpu.get_barrier_semaphore()
+    for off in range(1, n):
+        pl.semaphore_signal(
+            barrier, inc=1, device_id=(grp, lax.rem(me + off, n), core), device_id_type=MESH
+        )
+    pl.semaphore_signal(barrier, inc=1, device_id=(grp, me, other), device_id_type=MESH)
+
     weight_copies = []
     for h in range(2):
         span = pl.ds(h * half, half)
@@ -207,13 +214,6 @@
             )
     for i in (0, 3, 1, 4, 2, 5):
         weight_copies[i].start()
-
-    barrier = pltpu.get_barrier_semaphore()
-    for off in range(1, n):
-        pl.semaphore_signal(
-            barrier, inc=1, device_id=(grp, lax.rem(me + off, n), core), device_id_type=MESH
-        )
-    pl.semaphore_signal(barrier, inc=1, device_id=(grp, me, other), device_id_type=MESH)
 
     mine = pl.ds(pl.multiple_of(me * block, block), block)
     stage[...] = jnp.zeros_like(stage)

time: 38.3 us -> 37.2 us (0.971)
  Pallas kernels: 36.7 us -> 35.7 us
    pallas_call x1, Pallas kernels: 36.7 us -> 35.7 us  [fused_shards(): pl.pallas_call(functools.partial(fused_kernel, n), out_shape=jax.ShapeDty...]
where the time goes in v6:
time: 37.2 us; the launch traced here: 37 us
  Pallas kernels  35.7 us (96%)
  local copies, waits for them, and re-layouts  1.37 us (4%)
    pallas_call x1, Pallas kernels, fused_shards(): pl.pallas_call(functools.partial(fused_kernel, n), out_shape=jax.ShapeDty...  35.7 us
    unnamed x1, local copies, waits for them, and re-layouts  1.37 us

profile of v6, /device:TPU:0, one launch (start us, length us, event | category | flops | bytes accessed | tf_op | source)
XLA Modules:
  0.0 37.0 jit_solution(14096350075885021995)
XLA Ops:
  0.0 35.7 %shard_map.82 = bf16[4,3584]{1,0:T(4,128)(2,1)} custom-call(bf16[4,3584]{1,0:T(4,128)(2,1)} %hidden_hbm.1, s32[4]{0:T(128)} %place_hbm.1, s32[2,4,8]{2,1,0:T(4,128)} %ids_hbm.1, f32[2,4,8]{2,1,0:T(4,128)} %weights_hbm.1, f32[3584]{0:T(1024)} %gain_hbm.1, bf16[3584,512]{1,0:T(8,128)(2,1)} %wg_hbm.1, bf16[3584,512]{1,0:T(8,128)(2,1)} %wu_hbm.1, ...), custom_call_target="tpu_custom_call" | custom-call | flops 704643072 | bytes 11010048 | tf_op jit(solution)/shard_map/pallas_call | solution.py:436
  35.7 1.4 %copy.10 = bf16[4,3584]{1,0:T(4,128)(2,1)} copy(bf16[4,3584]{1,0:T(4,128)(2,1)} %shard_map.82) | data formatting | bytes 57344
